TPU v7x, 512 devices: a whole 4x4x16 slice. The times are simulated.
512 devices in a mesh: row: 16 (over y, x_hi, core), col: 32 (over x_lo, z).
Axes of the slice: x: 4 (x_hi: 2, x_lo: 2; x = x_hi * 2 + x_lo), y: 4, z: 16, core: 2. Of those that a mesh axis runs over, the one named last changes fastest.
Arguments:
- pair: bfloat16 [512, 512, 128], P('row', 'col'), may hold values from -6 to 6
- pair_mask: int32 [512, 512], P('row', 'col'), may hold values 0 or 1
- norm_gain: float32 [128], replicated, may hold values from 0.5 to 1.5
- norm_bias: float32 [128], replicated, may hold values from -3 to 3
- w_a_gate: bfloat16 [128, 128], replicated, may hold values from -0.5 to 0.5
- w_a_proj: bfloat16 [128, 128], replicated, may hold values from -0.5 to 0.5
- w_b_gate: bfloat16 [128, 128], replicated, may hold values from -0.5 to 0.5
- w_b_proj: bfloat16 [128, 128], replicated, may hold values from -0.5 to 0.5
- w_gate: bfloat16 [128, 128], replicated, may hold values from -0.5 to 0.5
- out_gain: float32 [128], replicated, may hold values from 0.5 to 1.5
- out_bias: float32 [128], replicated, may hold values from -3 to 3
- w_out: bfloat16 [128, 128], replicated, may hold values from -0.5 to 0.5
Outputs:
- update: bfloat16 [512, 512, 128], P('row', 'col')
All inputs are finite; a program needn't handle non-finite values. No bound on the sum of `pair_mask` on one device may be relied on, other than what follows from the above.
Results may differ from a plain program's by a relative error of at most 0.0054.
Values may be sent and summed in bfloat16 or wider, within the bound.
A program may use at most 64 MiB of HBM per device.

v0:
```python
import jax
import jax.numpy as jnp
from jax import lax
from jax.sharding import PartitionSpec as P


def broadcast(block, axis, holder):
    block = jnp.where(lax.axis_index(axis) == holder, block, jnp.zeros_like(block))
    return lax.psum(block, axis)


def layer_norm(values, gain, bias):
    mean = jnp.mean(values, axis=-1, keepdims=True)
    centred = values - mean
    variance = jnp.mean(centred * centred, axis=-1, keepdims=True)
    return centred * lax.rsqrt(variance + 1e-05) * gain + bias


def per_device(
    pair,
    pair_mask,
    norm_gain,
    norm_bias,
    w_a_gate,
    w_a_proj,
    w_b_gate,
    w_b_proj,
    w_gate,
    out_gain,
    out_bias,
    w_out,
):
    rows, cols, width = pair.shape
    normed = layer_norm(pair.astype(jnp.float32), norm_gain, norm_bias).astype(jnp.bfloat16)
    flat = normed.reshape(rows * cols, width)
    mask_col = pair_mask.astype(jnp.float32).reshape(rows * cols, 1)

    def project(weight):
        return jnp.dot(flat, weight, preferred_element_type=jnp.float32)

    right = (mask_col * jax.nn.sigmoid(project(w_b_gate)) * project(w_b_proj)).astype(jnp.bfloat16)
    hidden = right.shape[1]
    right = right.reshape(rows, cols, hidden)
    row_panel = lax.all_gather(right, "col", axis=1, tiled=True)
    ratio = rows // cols
    col_index = lax.axis_index("col")
    sub_block = col_index % ratio
    root_row = col_index // ratio
    picked = lax.dynamic_slice_in_dim(row_panel, sub_block * cols, cols, 0)
    right_rows = broadcast(picked, "row", root_row)
    left = (mask_col * jax.nn.sigmoid(project(w_a_gate)) * project(w_a_proj)).astype(jnp.bfloat16)
    left = left.reshape(rows, cols, hidden)
    gate = jax.nn.sigmoid(project(w_gate))
    contracted = jnp.einsum(
        "ikc,jkc->ijc",
        lax.all_gather(left, "col", axis=1, tiled=True),
        right_rows,
        preferred_element_type=jnp.float32,
    )
    normed_out = layer_norm(contracted, out_gain, out_bias).astype(jnp.bfloat16)
    result = gate * jnp.dot(
        normed_out.reshape(rows * cols, hidden), w_out, preferred_element_type=jnp.float32
    )
    return result.astype(jnp.bfloat16).reshape(rows, cols, width)


def solution(mesh):
    return jax.shard_map(
        per_device,
        mesh=mesh,
        in_specs=(
            P("row", "col", None),
            P("row", "col"),
            P(),
            P(),
            P(),
            P(),
            P(),
            P(),
            P(),
            P(),
            P(),
            P(),
        ),
        out_specs=P("row", "col", None),
        check_vma=False,
    )
```

profile of v0, /device:TPU:1, one launch (start us, length us, event | category | flops | bytes accessed | tf_op | source)
XLA Modules:
  0.0 579.0 jit_solution(5384596387194705834)
XLA Ops:
  6.5 1.1 convert_reduce_fusion
  7.6 0.1 copy.39
  7.7 0.1 copy.40
  7.8 1.1 fusion.16
  8.9 0.1 copy.41
  9.0 0.1 copy.42
  9.1 0.7 convert_element_type.23
  9.8 0.1 copy.43
  9.9 0.1 mul.71
  10.0 1.1 fusion.19
  11.1 0.2 fusion.7
  11.3 0.9 fusion.11
  12.3 0.7 copy.44
  13.0 0.2 fusion.3
  13.3 0.2 fusion.12
  13.5 1.2 copy.46
  14.8 124.3 %all-gather.3.cloned.1.call-done = bf16[32,512,128]{2,0,1:T(8,128)(2,1)} async-done(((bf16[32,16,128]{2,0,1:T(8,128)(2,1)}), bf16[32,512,128]{2,0,1:T(8,128)(2,1)}) %all-gather.3.cloned.1.call-update) | async-done | bytes 4194320 | tf_op jit(solution)/shard_map/all_gather | solution.py:44
  139.1 2.0 constant_dynamic-slice_fusion
  141.0 3.5 copy.54
  144.5 1.4 broadcast_select_fusion
  146.0 0.7 copy-done.6
  146.7 0.2 fusion.10
  147.0 235.7 %all-gather.5.cloned.1.call-done = bf16[32,512,128]{0,1,2:T(8,128)(2,1)} async-done(((bf16[32,16,128]{0,1,2:T(8,128)(2,1)}), bf16[32,512,128]{0,1,2:T(8,128)(2,1)}) %all-gather.5.cloned.1.call-update) | async-done | bytes 4194320 | tf_op jit(solution)/shard_map/all_gather | solution.py:56
  382.7 178.9 %all-reduce.2.cloned.1.call-done = bf16[16,512,128]{1,0,2:T(8,128)(2,1)} async-done(((bf16[16,512,128]{1,0,2:T(8,128)(2,1)}), bf16[16,512,128]{1,0,2:T(8,128)(2,1)}) %all-reduce.2.cloned.1.call-update) | async-done | bytes 2097168 | tf_op jit(solution)/shard_map/psum | solution.py:9
  561.6 8.8 %bitcast_reduce_fusion = (f32[32,16]{0,1:T(8,128)S(1)}, f32[128,16,32]{2,1,0:T(8,128)S(1)}) fusion(bf16[16,512,128]{1,0,2:T(8,128)(2,1)} %all-reduce.2.cloned.1.call-done, bf16[32,512,128]{0,1,2:T(8,128)(2,1)} %all-gather.5.cloned.1.call-done), kind=kOutput, calls=%fused_computation.21 | convolution fusion | flops 67173888 | bytes 6555648 | tf_op jit(solution)/shard_map/ikc,jkc->ijc/dot_general | solution.py:54
  570.4 0.5 copy.47
  570.9 0.1 copy.49
  571.0 0.2 multiply_reduce_fusion
  571.2 0.1 copy.53
  571.3 0.1 copy.51
  571.4 0.2 add_convert_fusion
  571.6 0.8 fusion.13
  (23 shorter events, 0.2 us)
Async XLA Ops:
  6.5 4.6 copy-start
  6.5 6.5 %copy-start.5 = (bf16[128,128]{1,0:T(8,128)(2,1)S(1)}, bf16[128,128]{1,0:T(8,128)(2,1)}, u32[]{:S(2)}) copy-start(bf16[128,128]{1,0:T(8,128)(2,1)} %param.16) | copy-start | bytes 98308
  6.5 6.7 %copy-start.1 = (bf16[128,128]{1,0:T(8,128)(2,1)S(1)}, bf16[128,128]{1,0:T(8,128)(2,1)}, u32[]{:S(2)}) copy-start(bf16[128,128]{1,0:T(8,128)(2,1)} %param.17) | copy-start | bytes 98308
  6.5 132.5 %all-gather.3.cloned.1.call-start = ((), (), s32[]{:S(2)}) async-start(), calls=%async_computation | async-start | bytes 4325376 | tf_op jit(solution)/shard_map/all_gather | solution.py:44
  13.0 369.7 %all-gather.5.cloned.1.call-start = ((), (), s32[]{:S(2)}) async-start(), calls=%async_computation.2 | async-start | bytes 17301504 | tf_op jit(solution)/shard_map/all_gather | solution.py:56
  14.7 546.9 %all-reduce.2.cloned.1.call-start = ((), (), s32[]{:S(2)}) async-start(), calls=%async_computation.1 | async-start | bytes 4194304 | tf_op jit(solution)/shard_map/psum | solution.py:9
  146.0 0.8 copy-start.6
  147.0 424.4 %copy-start.3 = (f32[128]{0:T(128)S(1)}, f32[128]{0:T(128)}, u32[]{:S(2)}) copy-start(f32[128]{0:T(128)} %param.22) | copy-start | bytes 1540
  147.0 424.4 %copy-start.4 = (f32[128]{0:T(128)S(1)}, f32[128]{0:T(128)}, u32[]{:S(2)}) copy-start(f32[128]{0:T(128)} %param.21) | copy-start | bytes 1540
  570.4 1.2 copy-start.2
Sparse Core Ops, SparseCore 0:
  13.1 125.9 all-gather.2
  141.1 241.6 all-gather.4
  385.7 175.8 all-reduce.1
where the time goes:
time: 579 us
  waiting for transfers between devices  539 us (93%)
  between operations  13.3 us (2%)
  matrix products  11.4 us (2%)
  local copies, waits for them, and re-layouts  9.3 us (2%)
  other arithmetic  5.98 us (1%)
    all_gather x1, waiting for transfers between devices, per_device(): lax.all_gather(left, 'col', axis=1, tiled=True)  236 us
    psum x1, waiting for transfers between devices, broadcast(): return lax.psum(block, axis)  179 us
    all_gather x1, waiting for transfers between devices, per_device(): row_panel = lax.all_gather(right, 'col', axis=1, tiled=True)  124 us
  transfers between devices with their start and end apart: 3, of which 3 were waited for; matrix products, arithmetic and copies ran while one was open for 2% of the time, Pallas kernels for 0%

commit v1 on v0

v1 whole, which is shorter than its diff:
```python
import jax
import jax.numpy as jnp
from jax import lax
from jax.experimental import pallas as pl
from jax.experimental.pallas import tpu as pltpu
from jax.sharding import PartitionSpec as P

MESH = pl.DeviceIdType.MESH
F32, BF16 = jnp.float32, jnp.bfloat16
NZ, NX, NY = 16, 4, 4
FAR_FIRST = (8, 7, 9, 6, 10, 5, 11, 4, 12, 3, 13, 2, 14, 1, 15)
PLANE = tuple((dy, dx) for dy in (2, 1, 3, 0) for dx in (2, 1, 3, 0) if dy or dx)
ALONG_X = (2, 1, 3)
NT = (((1,), (1,)), ((), ()))
TN = (((0,), (0,)), ((), ()))


def swap_blocks(arrays):
    arrays = list(arrays)
    lane = lax.broadcasted_iota(jnp.int32, arrays[0].shape, 1)
    for bit in range(3):
        step = 1 << bit
        upper = ((lane // 16) // step) % 2 == 1
        for a in range(8):
            if not a & step:
                low, high = arrays[a], arrays[a | step]
                arrays[a] = jnp.where(upper, pltpu.roll(high, 16 * step, 1), low)
                arrays[a | step] = jnp.where(upper, high, pltpu.roll(low, 128 - 16 * step, 1))
    return arrays


def kernel(
    pair_hbm, mask_hbm, norm_gain_hbm, norm_bias_hbm, w_a_gate_hbm, w_a_proj_hbm, w_b_gate_hbm, w_b_proj_hbm,
    w_gate_hbm, out_gain_hbm, out_bias_hbm, w_out_hbm,
    out_ref,
    pair, mask, norm_gain, norm_bias, w_a_gate, w_a_proj, w_b_gate, w_b_proj, w_gate, out_gain, out_bias, w_out,
    normed, gate, z_send, z_recv, turned, edges, shared, left_all, right_all, product, product_x, turned_back,
    back_send, back_recv,
    in_sem, z_ss, z_rs, core_ss, core_rs, right_ss, right_rs, left_ss, left_rs, x_ss, x_rs, back_ss, back_rs, local_sem,
):
    row, col = lax.axis_index("row"), lax.axis_index("col")
    y, core = row // 4, row % 2
    x = ((row // 2) % 2) * 2 + col // 16
    z = col % 16

    def device(y, x, core, z):
        return {"row": y * 4 + (x // 2) * 2 + core, "col": (x % 2) * 16 + z}

    z_peers = [device(y, x, core, (z + d) % NZ) for d in FAR_FIRST]
    plane_peers = [device((y + dy) % NY, (x + dx) % NX, core, z) for dy, dx in PLANE]
    other_core = device(y, x, 1 - core, z)
    x_other_core = [device(y, (x + dx) % NX, 1 - core, z) for dx in ALONG_X]
    barrier = pltpu.get_barrier_semaphore()
    peers = z_peers + plane_peers + [other_core] + x_other_core
    for peer in peers:
        pl.semaphore_signal(barrier, inc=1, device_id=peer, device_id_type=MESH)

    hbm = (pair_hbm, mask_hbm, norm_gain_hbm, norm_bias_hbm, w_a_gate_hbm, w_a_proj_hbm, w_b_gate_hbm, w_b_proj_hbm,
           w_gate_hbm, out_gain_hbm, out_bias_hbm, w_out_hbm)
    vmem = (pair, mask, norm_gain, norm_bias, w_a_gate, w_a_proj, w_b_gate, w_b_proj, w_gate, out_gain, out_bias, w_out)
    loads = [pltpu.make_async_copy(src, dst, in_sem.at[n]) for n, (src, dst) in enumerate(zip(hbm, vmem))]
    for load in loads:
        load.start()
    for load in loads:
        load.wait()

    values = pair[...].astype(F32).reshape(512, 128)
    centred = values - jnp.mean(values, axis=1, keepdims=True)
    variance = jnp.mean(centred * centred, axis=1, keepdims=True)
    normed[...] = (centred * lax.rsqrt(variance + 1e-05) * norm_gain[...] + norm_bias[...]).astype(BF16)

    at_col = lax.broadcasted_iota(jnp.int32, (16, 512), 1) % 16 == lax.broadcasted_iota(jnp.int32, (16, 512), 0)
    at_row = lax.broadcasted_iota(jnp.int32, (32, 512), 1) // 16 == lax.broadcasted_iota(jnp.int32, (32, 512), 0)
    spread = lax.dot_general(
        mask[...].astype(F32).astype(BF16), at_col.astype(F32).astype(BF16), TN, preferred_element_type=F32
    )
    mask_row = jnp.sum(jnp.where(at_row, spread, 0.0), axis=0, keepdims=True)

    def project(weight):
        turned_weight = weight[...].astype(F32).T.astype(BF16)
        return lax.dot_general(turned_weight, normed[...], NT, preferred_element_type=F32)

    left = mask_row * jax.nn.sigmoid(project(w_a_gate)) * project(w_a_proj)
    right = mask_row * jax.nn.sigmoid(project(w_b_gate)) * project(w_b_proj)
    for part in range(4):
        lanes = slice(part * 128, part * 128 + 128)
        both = jnp.concatenate([left[:, lanes].reshape(16, 8, 128), right[:, lanes].reshape(16, 8, 128)], axis=1)
        z_send[:, part * 16 : part * 16 + 16, :] = both.astype(BF16)

    pl.semaphore_wait(barrier, len(peers))

    z_copies = []
    for n, d in enumerate(FAR_FIRST):
        copy = pltpu.make_async_remote_copy(
            src_ref=z_send.at[(z + d) % NZ], dst_ref=z_recv.at[d], send_sem=z_ss.at[d], recv_sem=z_rs.at[d],
            device_id=z_peers[n], device_id_type=MESH,
        )
        copy.start()
        z_copies.append(copy)
    own = pltpu.make_async_copy(z_send.at[z], z_recv.at[0], local_sem.at[0])
    own.start()

    gate[...] = jax.nn.sigmoid(jnp.dot(normed[...], w_gate[...], preferred_element_type=F32))

    own.wait()
    for copy in z_copies:
        copy.wait_recv()

    for half in range(2):
        blocks = swap_blocks([z_recv[half * 8 + a].astype(F32) for a in range(8)])
        for low in range(8):
            turned[half, low * 64 : low * 64 + 64, :] = blocks[low]
    for side in range(2):
        for channel in range(8):
            halves = []
            for half in range(2):
                rows = [turned[half, pl.ds(part * 16 + side * 8 + channel, 8, stride=64), :] for part in range(4)]
                halves.append(jnp.concatenate(rows, axis=0))
            edges[channel // 4, side, channel % 4] = jnp.concatenate(halves, axis=1).astype(BF16)

    swap = pltpu.make_async_remote_copy(
        src_ref=edges.at[1 - core], dst_ref=shared.at[:, :, pl.ds(pl.multiple_of(core * 32, 32), 32), :],
        send_sem=core_ss, recv_sem=core_rs, device_id=other_core, device_id_type=MESH,
    )
    swap.start()
    keep = pltpu.make_async_copy(
        edges.at[core], shared.at[:, :, pl.ds(pl.multiple_of(core * 32, 32), 32), :], local_sem.at[1]
    )
    keep.start()
    keep.wait()
    swap.wait_recv()

    right_copies, left_copies = [], []
    right_rows = pl.ds(pl.multiple_of((y * 2 + x // 2) * 64, 64), 64)
    left_rows = pl.ds(pl.multiple_of((x // 2) * 64, 64), 64)
    for n, (dy, dx) in enumerate(PLANE):
        copy = pltpu.make_async_remote_copy(
            src_ref=shared.at[1, (x + dx) % NX], dst_ref=right_all.at[x % 2, right_rows, :],
            send_sem=right_ss.at[n], recv_sem=right_rs.at[n], device_id=plane_peers[n], device_id_type=MESH,
        )
        copy.start()
        right_copies.append(copy)
    for n, dx in enumerate(ALONG_X):
        copy = pltpu.make_async_remote_copy(
            src_ref=shared.at[0, (x + dx) % NX], dst_ref=left_all.at[x % 2, left_rows, :],
            send_sem=left_ss.at[n], recv_sem=left_rs.at[n], device_id=device(y, (x + dx) % NX, core, z),
            device_id_type=MESH,
        )
        copy.start()
        left_copies.append(copy)
    own_right = pltpu.make_async_copy(shared.at[1, x], right_all.at[x % 2, right_rows, :], local_sem.at[2])
    own_left = pltpu.make_async_copy(shared.at[0, x], left_all.at[x % 2, left_rows, :], local_sem.at[3])
    own_right.start()
    own_left.start()
    own_right.wait()
    own_left.wait()
    for n, dx in enumerate(ALONG_X):
        source = (x + NX - dx) % NX
        rows = pl.ds(pl.multiple_of((source // 2) * 64, 64), 64)
        pltpu.make_async_remote_copy(
            src_ref=shared.at[0, 0], dst_ref=left_all.at[source % 2, rows, :],
            send_sem=left_ss.at[n], recv_sem=left_rs.at[n], device_id=other_core, device_id_type=MESH,
        ).wait_recv()
    for n, (dy, dx) in enumerate(PLANE):
        source_y, source_x = (y + NY - dy) % NY, (x + NX - dx) % NX
        rows = pl.ds(pl.multiple_of((source_y * 2 + source_x // 2) * 64, 64), 64)
        pltpu.make_async_remote_copy(
            src_ref=shared.at[1, 0], dst_ref=right_all.at[source_x % 2, rows, :],
            send_sem=right_ss.at[n], recv_sem=right_rs.at[n], device_id=other_core, device_id_type=MESH,
        ).wait_recv()

    for half in range(2):
        total = lax.dot_general(
            left_all[0], right_all[0, half * 256 : half * 256 + 256, :], NT, preferred_element_type=F32
        ) + lax.dot_general(
            left_all[1], right_all[1, half * 256 : half * 256 + 256, :], NT, preferred_element_type=F32
        )
        product[half] = total.astype(BF16)

    x_copies = []
    slot = core * 4 + x
    for n, (dx, dc) in enumerate([(dx, dc) for dx in ALONG_X + (0,) for dc in (1, 0) if dx or dc]):
        to_x = (x + dx) % NX
        to_core = (core + dc) % 2
        rows = pl.ds(pl.multiple_of(((to_x // 2) * 2 + to_core) * 32, 32), 32)
        copy = pltpu.make_async_remote_copy(
            src_ref=product.at[to_x % 2, rows, :], dst_ref=product_x.at[slot],
            send_sem=x_ss.at[n], recv_sem=x_rs.at[n], device_id=device(y, to_x, to_core, z), device_id_type=MESH,
        )
        copy.start()
        x_copies.append((copy, dx, dc))
    rows = pl.ds(pl.multiple_of(((x // 2) * 2 + core) * 32, 32), 32)
    own_product = pltpu.make_async_copy(product.at[x % 2, rows, :], product_x.at[slot], local_sem.at[4])
    own_product.start()
    own_product.wait()
    for n, (copy, dx, dc) in enumerate(x_copies):
        source = ((core + dc) % 2) * 4 + (x + NX - dx) % NX
        pltpu.make_async_remote_copy(
            src_ref=product.at[0, pl.ds(0, 32), :], dst_ref=product_x.at[source],
            send_sem=x_ss.at[n], recv_sem=x_rs.at[n], device_id=other_core, device_id_type=MESH,
        ).wait_recv()

    for half in range(2):
        for channel in range(8):
            turned_back[half, channel * 32 : channel * 32 + 32, :] = product_x[
                channel, :, half * 128 : half * 128 + 128
            ].astype(F32)
    for half in range(2):
        rows = []
        for low in range(8):
            rows.append(
                jnp.concatenate(
                    [turned_back[half, pl.ds(part * 8 + low, 8, stride=32), :] for part in range(4)], axis=0
                )
            )
        for low, block in enumerate(swap_blocks(rows)):
            back_send[half * 8 + low] = block.astype(BF16)

    back_copies = []
    for n, d in enumerate(FAR_FIRST):
        copy = pltpu.make_async_remote_copy(
            src_ref=back_send.at[(z + d) % NZ], dst_ref=back_recv.at[z], send_sem=back_ss.at[d], recv_sem=back_rs.at[d],
            device_id=z_peers[n], device_id_type=MESH,
        )
        copy.start()
        back_copies.append(copy)
    own_back = pltpu.make_async_copy(back_send.at[z], back_recv.at[z], local_sem.at[5])
    own_back.start()
    own_back.wait()
    for n, d in enumerate(FAR_FIRST):
        pltpu.make_async_remote_copy(
            src_ref=back_send.at[0], dst_ref=back_recv.at[(z + NZ - d) % NZ], send_sem=back_ss.at[d],
            recv_sem=back_rs.at[d], device_id=other_core, device_id_type=MESH,
        ).wait_recv()

    gain_col = jnp.broadcast_to(out_gain[...], (8, 128)).T[:, :1]
    bias_col = jnp.broadcast_to(out_bias[...], (8, 128)).T[:, :1]
    gathered = back_recv[...].astype(F32)
    for part in range(4):
        contracted = gathered[:, part * 8 : part * 8 + 8, :].reshape(128, 128)
        centred = contracted - jnp.mean(contracted, axis=0, keepdims=True)
        variance = jnp.mean(centred * centred, axis=0, keepdims=True)
        normed_out = (centred * lax.rsqrt(variance + 1e-05) * gain_col + bias_col).T.astype(BF16)
        result = gate[part * 128 : part * 128 + 128, :] * jnp.dot(normed_out, w_out[...], preferred_element_type=F32)
        out_ref[part * 8 : part * 8 + 8] = result.astype(BF16).reshape(8, 16, 128)

    for copy in z_copies + [swap] + right_copies + left_copies + [c for c, _, _ in x_copies] + back_copies:
        copy.wait_send()


def per_device(
    pair, pair_mask, norm_gain, norm_bias, w_a_gate, w_a_proj, w_b_gate, w_b_proj, w_gate, out_gain, out_bias, w_out
):
    args = (
        pair, pair_mask.T, norm_gain.reshape(1, 128), norm_bias.reshape(1, 128), w_a_gate, w_a_proj, w_b_gate, w_b_proj,
        w_gate, out_gain.reshape(1, 128), out_bias.reshape(1, 128), w_out,
    )
    dma = pltpu.SemaphoreType.DMA
    return pl.pallas_call(
        kernel,
        out_shape=jax.ShapeDtypeStruct(pair.shape, BF16),
        in_specs=[pl.BlockSpec(memory_space=pl.ANY)] * len(args),
        out_specs=pl.BlockSpec(memory_space=pltpu.VMEM),
        scratch_shapes=[pltpu.VMEM(a.shape, a.dtype) for a in args]
        + [
            pltpu.VMEM((512, 128), BF16),
            pltpu.VMEM((512, 128), F32),
            pltpu.VMEM((16, 64, 128), BF16),
            pltpu.VMEM((16, 64, 128), BF16),
            pltpu.VMEM((2, 512, 128), F32),
            pltpu.VMEM((2, 2, 4, 32, 256), BF16),
            pltpu.VMEM((2, 4, 64, 256), BF16),
            pltpu.VMEM((2, 128, 256), BF16),
            pltpu.VMEM((2, 512, 256), BF16),
            pltpu.VMEM((2, 128, 256), BF16),
            pltpu.VMEM((8, 32, 256), BF16),
            pltpu.VMEM((2, 256, 128), F32),
            pltpu.VMEM((16, 32, 128), BF16),
            pltpu.VMEM((16, 32, 128), BF16),
            dma((12,)), dma((16,)), dma((16,)), dma(()), dma(()), dma((15,)), dma((15,)), dma((3,)), dma((3,)),
            dma((7,)), dma((7,)), dma((16,)), dma((16,)), dma((6,)),
        ],
        compiler_params=pltpu.CompilerParams(collective_id=0, has_side_effects=True, vmem_limit_bytes=60 << 20),
        name="triangle",
    )(*args)


def solution(mesh):
    return jax.shard_map(
        per_device,
        mesh=mesh,
        in_specs=(P("row", "col", None), P("row", "col")) + (P(),) * 10,
        out_specs=P("row", "col", None),
        check_vma=False,
    )
```

time: 579 us -> 57.7 us (0.10)
  the two profiles are of different devices: /device:TPU:1 before, /device:TPU:16 now
where the time goes in v1:
time: 57.7 us; the launch traced here: 57.6 us
  Pallas kernels  56 us (97%)
  local copies, waits for them, and re-layouts  1.57 us (3%)
    pallas_call x1, Pallas kernels, per_device(): pl.pallas_call(kernel, out_shape=jax.ShapeDtypeStruct(pair.shape, BF16),...  56 us
    unnamed x1, local copies, waits for them, and re-layouts  1.57 us

profile of v1, /device:TPU:16, one launch (start us, length us, event | category | flops | bytes accessed | tf_op | source)
XLA Modules:
  0.0 57.6 jit_solution(8774538316042828243)
XLA Ops:
  0.0 56.0 %triangle.1 = bf16[32,16,128]{2,1,0:T(8,128)(2,1)} custom-call(bf16[32,16,128]{2,1,0:T(8,128)(2,1)} %pair_hbm.1, s32[16,32]{1,0:T(8,128)} %bitcast.5, f32[1,128]{1,0:T(1,128)} %bitcast.6, f32[1,128]{1,0:T(1,128)} %bitcast.7, bf16[128,128]{1,0:T(8,128)(2,1)} %w_a_gate_hbm.1, bf16[128,128]{1,0:T(8,128)(2,1)} %w_a_proj_hbm.1, bf16[128,128]{1,0:T(8,128)(2,1)} %w_b_gate_hbm.1, ...), custom_call_target="tpu_custom_call" | custom-call | tf_op jit(solution)/shard_map/triangle/pallas_call | solution.py:259
  56.0 1.6 %copy.14 = bf16[32,16,128]{2,1,0:T(8,128)(2,1)} copy(bf16[32,16,128]{2,1,0:T(8,128)(2,1)} %triangle.1) | data formatting | bytes 262144

commit v2 on v1

v2 whole, which is shorter than its diff:
```python
import jax
import jax.numpy as jnp
from jax import lax
from jax.experimental import pallas as pl
from jax.experimental.pallas import tpu as pltpu
from jax.sharding import PartitionSpec as P

MESH = pl.DeviceIdType.MESH
F32, BF16 = jnp.float32, jnp.bfloat16
NZ, NX, NY = 16, 4, 4
FAR_FIRST = (8, 7, 9, 6, 10, 5, 11, 4, 12, 3, 13, 2, 14, 1, 15)
PLANE = tuple((dy, dx) for dy in (2, 1, 3, 0) for dx in (2, 1, 3, 0) if dy or dx)
ALONG_X = (2, 1, 3)
X_AND_CORE = tuple((dx, dc) for dx in ALONG_X + (0,) for dc in (1, 0) if dx or dc)
NT = (((1,), (1,)), ((), ()))
TN = (((0,), (0,)), ((), ()))


def swap_blocks(arrays):
    arrays = list(arrays)
    lane = lax.broadcasted_iota(jnp.int32, arrays[0].shape, 1)
    for bit in range(3):
        step = 1 << bit
        upper = ((lane // 16) // step) % 2 == 1
        for a in range(8):
            if not a & step:
                low, high = arrays[a], arrays[a | step]
                arrays[a] = jnp.where(upper, pltpu.roll(high, 16 * step, 1), low)
                arrays[a | step] = jnp.where(upper, high, pltpu.roll(low, 128 - 16 * step, 1))
    return arrays


def kernel(
    pair_hbm, mask_hbm, norm_gain_hbm, norm_bias_hbm, w_a_gate_hbm, w_a_proj_hbm, w_b_gate_hbm, w_b_proj_hbm,
    w_gate_hbm, out_gain_hbm, out_bias_hbm, w_out_hbm,
    out_ref,
    pair, mask, norm_gain, norm_bias, w_a_gate, w_a_proj, w_b_gate, w_b_proj, w_gate, out_gain, out_bias, w_out,
    normed, gate, z_send, z_recv, turned, left_edges, right_edges, shared, left_all, right_all, product, product_x,
    turned_back, back_send, back_recv,
    in_sem, z_ss, z_rs, core_ss, core_rs, right_ss, right_rs, left_ss, left_rs, x_ss, x_rs, back_ss, back_rs, local_sem,
):
    row, col = lax.axis_index("row"), lax.axis_index("col")
    y, core = row // 4, row % 2
    x = ((row // 2) % 2) * 2 + col // 16
    z = col % 16

    def device(y, x, core, z):
        return {"row": y * 4 + (x // 2) * 2 + core, "col": (x % 2) * 16 + z}

    def remote(src, dst, ss, rs, to):
        return pltpu.make_async_remote_copy(
            src_ref=src, dst_ref=dst, send_sem=ss, recv_sem=rs, device_id=to, device_id_type=MESH
        )

    z_peers = [device(y, x, core, (z + d) % NZ) for d in FAR_FIRST]
    plane_peers = [device((y + dy) % NY, (x + dx) % NX, core, z) for dy, dx in PLANE]
    other_core = device(y, x, 1 - core, z)
    x_other_core = [device(y, (x + dx) % NX, 1 - core, z) for dx in ALONG_X]
    barrier = pltpu.get_barrier_semaphore()
    peers = z_peers + plane_peers + [other_core] + x_other_core
    for peer in peers:
        pl.semaphore_signal(barrier, inc=1, device_id=peer, device_id_type=MESH)

    loads = [
        pltpu.make_async_copy(src, dst, in_sem.at[n])
        for n, (src, dst) in enumerate(
            (
                (pair_hbm, pair), (norm_gain_hbm, norm_gain), (norm_bias_hbm, norm_bias), (w_b_gate_hbm, w_b_gate),
                (w_b_proj_hbm, w_b_proj), (mask_hbm, mask), (w_a_gate_hbm, w_a_gate), (w_a_proj_hbm, w_a_proj),
                (w_gate_hbm, w_gate), (out_gain_hbm, out_gain), (out_bias_hbm, out_bias), (w_out_hbm, w_out),
            )
        )
    ]
    for load in loads:
        load.start()
    for load in loads[:6]:
        load.wait()

    values = pair[...].astype(F32).reshape(512, 128)
    centred = values - jnp.mean(values, axis=1, keepdims=True)
    variance = jnp.mean(centred * centred, axis=1, keepdims=True)
    normed[...] = (centred * lax.rsqrt(variance + 1e-05) * norm_gain[...] + norm_bias[...]).astype(BF16)

    at_col = lax.broadcasted_iota(jnp.int32, (16, 512), 1) % 16 == lax.broadcasted_iota(jnp.int32, (16, 512), 0)
    at_row = lax.broadcasted_iota(jnp.int32, (32, 512), 1) // 16 == lax.broadcasted_iota(jnp.int32, (32, 512), 0)
    spread = lax.dot_general(
        mask[...].astype(F32).astype(BF16), at_col.astype(F32).astype(BF16), TN, preferred_element_type=F32
    )
    mask_row = jnp.sum(jnp.where(at_row, spread, 0.0), axis=0, keepdims=True)

    def project(weight):
        turned_weight = weight[...].astype(F32).T.astype(BF16)
        return lax.dot_general(turned_weight, normed[...], NT, preferred_element_type=F32)

    def edges_of(side, w_gate, w_proj):
        edges = mask_row * jax.nn.sigmoid(project(w_gate)) * project(w_proj)
        parts = [edges[:, part * 128 : part * 128 + 128].reshape(16, 8, 128) for part in range(4)]
        z_send[side] = jnp.concatenate(parts, axis=1).astype(BF16)

    def start_along_z(side):
        copies = [
            remote(z_send.at[side, (z + d) % NZ], z_recv.at[side, d], z_ss.at[side, d], z_rs.at[side, d], z_peers[n])
            for n, d in enumerate(FAR_FIRST)
        ]
        for copy in copies:
            copy.start()
        own = pltpu.make_async_copy(z_send.at[side, z], z_recv.at[side, 0], local_sem.at[side])
        own.start()
        return own, copies

    def finish_along_z(side, own, copies):
        own.wait()
        for copy in copies:
            copy.wait_recv()
        for half in range(2):
            blocks = swap_blocks([z_recv[side, half * 8 + a].astype(F32) for a in range(8)])
            for low in range(8):
                turned[side, half, low * 32 : low * 32 + 32, :] = blocks[low]

    def channel_rows(side, channel):
        halves = []
        for half in range(2):
            rows = [turned[side, half, pl.ds(part * 8 + channel, 8, stride=32), :] for part in range(4)]
            halves.append(jnp.concatenate(rows, axis=0))
        return jnp.concatenate(halves, axis=1).astype(BF16)

    edges_of(1, w_b_gate, w_b_proj)
    pl.semaphore_wait(barrier, len(peers))
    right_own, right_z = start_along_z(1)
    for load in loads[6:]:
        load.wait()
    edges_of(0, w_a_gate, w_a_proj)
    left_own, left_z = start_along_z(0)
    gate[...] = jax.nn.sigmoid(jnp.dot(normed[...], w_gate[...], preferred_element_type=F32))

    finish_along_z(1, right_own, right_z)
    for channel in range(8):
        right_edges[channel // 4, channel % 4] = channel_rows(1, channel)
    own_rows = pl.ds(pl.multiple_of(core * 32, 32), 32)
    swap = remote(right_edges.at[1 - core], shared.at[:, own_rows, :], core_ss, core_rs, other_core)
    swap.start()
    keep = pltpu.make_async_copy(right_edges.at[core], shared.at[:, own_rows, :], local_sem.at[2])
    keep.start()
    keep.wait()
    swap.wait_recv()

    def right_rows(y, x):
        return right_all.at[x % 2, pl.ds(pl.multiple_of((y * 2 + x // 2) * 64, 64), 64), :]

    right_copies = [
        remote(shared.at[(x + dx) % NX], right_rows(y, x), right_ss.at[n], right_rs.at[n], plane_peers[n])
        for n, (dy, dx) in enumerate(PLANE)
    ]
    for copy in right_copies:
        copy.start()
    own_right = pltpu.make_async_copy(shared.at[x], right_rows(y, x), local_sem.at[3])
    own_right.start()

    finish_along_z(0, left_own, left_z)
    for channel in range(8):
        left_edges[channel] = channel_rows(0, channel)

    def left_rows(x, core):
        return left_all.at[x % 2, pl.ds(pl.multiple_of(((x // 2) * 2 + core) * 32, 32), 32), :]

    left_copies = []
    for n, (dx, dc) in enumerate(X_AND_CORE):
        to_x, to_core = (x + dx) % NX, (core + dc) % 2
        copy = remote(
            left_edges.at[to_core * 4 + to_x], left_rows(x, core), left_ss.at[n], left_rs.at[n],
            device(y, to_x, to_core, z),
        )
        copy.start()
        left_copies.append(copy)
    own_left = pltpu.make_async_copy(left_edges.at[core * 4 + x], left_rows(x, core), local_sem.at[4])
    own_left.start()
    own_right.wait()
    own_left.wait()
    for n, (dy, dx) in enumerate(PLANE):
        arrived = right_rows((y + NY - dy) % NY, (x + NX - dx) % NX)
        remote(shared.at[0], arrived, right_ss.at[n], right_rs.at[n], other_core).wait_recv()
    for n, (dx, dc) in enumerate(X_AND_CORE):
        arrived = left_rows((x + NX - dx) % NX, (core + dc) % 2)
        remote(left_edges.at[0], arrived, left_ss.at[n], left_rs.at[n], other_core).wait_recv()

    for half in range(2):
        total = lax.dot_general(
            left_all[0], right_all[0, half * 256 : half * 256 + 256, :], NT, preferred_element_type=F32
        ) + lax.dot_general(
            left_all[1], right_all[1, half * 256 : half * 256 + 256, :], NT, preferred_element_type=F32
        )
        product[half] = total.astype(BF16)

    def product_rows(x, core):
        return product.at[x % 2, pl.ds(pl.multiple_of(((x // 2) * 2 + core) * 32, 32), 32), :]

    x_copies = []
    for n, (dx, dc) in enumerate(X_AND_CORE):
        to_x, to_core = (x + dx) % NX, (core + dc) % 2
        copy = remote(
            product_rows(to_x, to_core), product_x.at[core * 4 + x], x_ss.at[n], x_rs.at[n], device(y, to_x, to_core, z)
        )
        copy.start()
        x_copies.append(copy)
    own_product = pltpu.make_async_copy(product_rows(x, core), product_x.at[core * 4 + x], local_sem.at[5])
    own_product.start()
    own_product.wait()
    for n, (dx, dc) in enumerate(X_AND_CORE):
        arrived = product_x.at[((core + dc) % 2) * 4 + (x + NX - dx) % NX]
        remote(product_rows(0, 0), arrived, x_ss.at[n], x_rs.at[n], other_core).wait_recv()

    for half in range(2):
        for channel in range(8):
            turned_back[half, channel * 32 : channel * 32 + 32, :] = product_x[
                channel, :, half * 128 : half * 128 + 128
            ].astype(F32)
    for half in range(2):
        rows = []
        for low in range(8):
            rows.append(
                jnp.concatenate(
                    [turned_back[half, pl.ds(part * 8 + low, 8, stride=32), :] for part in range(4)], axis=0
                )
            )
        for low, block in enumerate(swap_blocks(rows)):
            back_send[half * 8 + low] = block.astype(BF16)

    back_copies = [
        remote(back_send.at[(z + d) % NZ], back_recv.at[z], back_ss.at[d], back_rs.at[d], z_peers[n])
        for n, d in enumerate(FAR_FIRST)
    ]
    for copy in back_copies:
        copy.start()
    own_back = pltpu.make_async_copy(back_send.at[z], back_recv.at[z], local_sem.at[6])
    own_back.start()
    own_back.wait()
    for d in FAR_FIRST:
        arrived = back_recv.at[(z + NZ - d) % NZ]
        remote(back_send.at[0], arrived, back_ss.at[d], back_rs.at[d], other_core).wait_recv()

    gain_col = jnp.broadcast_to(out_gain[...], (8, 128)).T[:, :1]
    bias_col = jnp.broadcast_to(out_bias[...], (8, 128)).T[:, :1]
    gathered = back_recv[...].astype(F32)
    for part in range(4):
        contracted = gathered[:, part * 8 : part * 8 + 8, :].reshape(128, 128)
        centred = contracted - jnp.mean(contracted, axis=0, keepdims=True)
        variance = jnp.mean(centred * centred, axis=0, keepdims=True)
        normed_out = (centred * lax.rsqrt(variance + 1e-05) * gain_col + bias_col).T.astype(BF16)
        result = gate[part * 128 : part * 128 + 128, :] * jnp.dot(normed_out, w_out[...], preferred_element_type=F32)
        out_ref[part * 8 : part * 8 + 8] = result.astype(BF16).reshape(8, 16, 128)

    for copy in right_z + left_z + [swap] + right_copies + left_copies + x_copies + back_copies:
        copy.wait_send()


def per_device(
    pair, pair_mask, norm_gain, norm_bias, w_a_gate, w_a_proj, w_b_gate, w_b_proj, w_gate, out_gain, out_bias, w_out
):
    args = (
        pair, pair_mask.T, norm_gain.reshape(1, 128), norm_bias.reshape(1, 128), w_a_gate, w_a_proj, w_b_gate, w_b_proj,
        w_gate, out_gain.reshape(1, 128), out_bias.reshape(1, 128), w_out,
    )
    dma = pltpu.SemaphoreType.DMA
    return pl.pallas_call(
        kernel,
        out_shape=pltpu.VMEM(pair.shape, BF16),
        in_specs=[pl.BlockSpec(memory_space=pl.ANY)] * len(args),
        out_specs=pl.BlockSpec(memory_space=pltpu.VMEM),
        scratch_shapes=[pltpu.VMEM(a.shape, a.dtype) for a in args]
        + [
            pltpu.VMEM((512, 128), BF16),
            pltpu.VMEM((512, 128), F32),
            pltpu.VMEM((2, 16, 32, 128), BF16),
            pltpu.VMEM((2, 16, 32, 128), BF16),
            pltpu.VMEM((2, 2, 256, 128), F32),
            pltpu.VMEM((8, 32, 256), BF16),
            pltpu.VMEM((2, 4, 32, 256), BF16),
            pltpu.VMEM((4, 64, 256), BF16),
            pltpu.VMEM((2, 128, 256), BF16),
            pltpu.VMEM((2, 512, 256), BF16),
            pltpu.VMEM((2, 128, 256), BF16),
            pltpu.VMEM((8, 32, 256), BF16),
            pltpu.VMEM((2, 256, 128), F32),
            pltpu.VMEM((16, 32, 128), BF16),
            pltpu.VMEM((16, 32, 128), BF16),
            dma((12,)), dma((2, 16)), dma((2, 16)), dma(()), dma(()), dma((15,)), dma((15,)), dma((7,)), dma((7,)),
            dma((7,)), dma((7,)), dma((16,)), dma((16,)), dma((7,)),
        ],
        compiler_params=pltpu.CompilerParams(collective_id=0, has_side_effects=True, vmem_limit_bytes=32 << 20),
        name="triangle",
    )(*[pltpu.with_memory_space_constraint(a, pltpu.HBM) for a in args])


def solution(mesh):
    return jax.shard_map(
        per_device,
        mesh=mesh,
        in_specs=(P("row", "col", None), P("row", "col")) + (P(),) * 10,
        out_specs=P("row", "col", None),
        check_vma=False,
    )
```

time: 57.7 us -> 52.7 us (0.913)
  the two profiles are of different devices: /device:TPU:16 before, /device:TPU:1 now
where the time goes in v2:
time: 52.7 us; the launch traced here: 52.6 us
  Pallas kernels  51.9 us (98%)
  local copies, waits for them, and re-layouts  0.66 us (1%)
    pallas_call x1, Pallas kernels, per_device(): pl.pallas_call(kernel, out_shape=pltpu.VMEM(pair.shape, BF16), in_specs=[...  51.9 us

profile of v2, /device:TPU:1, one launch (start us, length us, event | category | flops | bytes accessed | tf_op | source)
XLA Modules:
  0.0 52.6 jit_solution(2375234881169070745)
XLA Ops:
  0.0 51.9 %triangle.1 = bf16[32,16,128]{2,1,0:T(8,128)(2,1)S(1)} custom-call(bf16[32,16,128]{2,1,0:T(8,128)(2,1)} %pair_hbm.1, s32[16,32]{1,0:T(8,128)} %bitcast.5, f32[1,128]{1,0:T(1,128)} %bitcast.6, f32[1,128]{1,0:T(1,128)} %bitcast.7, bf16[128,128]{1,0:T(8,128)(2,1)} %w_a_gate_hbm.1, bf16[128,128]{1,0:T(8,128)(2,1)} %w_a_proj_hbm.1, ...), custom_call_target="tpu_custom_call" | custom-call | tf_op jit(solution)/shard_map/triangle/pallas_call | solution.py:264
  51.9 0.7 %copy.14 = bf16[32,16,128]{2,1,0:T(8,128)(2,1)} copy(bf16[32,16,128]{2,1,0:T(8,128)(2,1)S(1)} %triangle.1) | data formatting | bytes 262144

commit v3 on v2

v3 whole, which is shorter than its diff:
```python
import jax
import jax.numpy as jnp
from jax import lax
from jax.experimental import pallas as pl
from jax.experimental.pallas import tpu as pltpu
from jax.sharding import PartitionSpec as P

MESH = pl.DeviceIdType.MESH
F32, BF16 = jnp.float32, jnp.bfloat16
NZ, NX, NY = 16, 4, 4
FAR_FIRST = (8, 7, 9, 6, 10, 5, 11, 4, 12, 3, 13, 2, 14, 1, 15)
NEAR = (4, 12, 3, 13, 2, 14, 1, 15)
ALONG_Y = (2, 1, 3)
X_AND_CORE = tuple((dx, dc) for dx in (2, 1, 3, 0) for dc in (1, 0) if dx or dc)
NT = (((1,), (1,)), ((), ()))
TN = (((0,), (0,)), ((), ()))


def swap_blocks(arrays):
    arrays = list(arrays)
    lane = lax.broadcasted_iota(jnp.int32, arrays[0].shape, 1)
    for bit in range(3):
        step = 1 << bit
        upper = ((lane // 16) // step) % 2 == 1
        for a in range(8):
            if not a & step:
                low, high = arrays[a], arrays[a | step]
                arrays[a] = jnp.where(upper, pltpu.roll(high, 16 * step, 1), low)
                arrays[a | step] = jnp.where(upper, high, pltpu.roll(low, 128 - 16 * step, 1))
    return arrays


def kernel(
    pair_hbm, mask_hbm, norm_gain_hbm, norm_bias_hbm, w_a_gate_hbm, w_a_proj_hbm, w_b_gate_hbm, w_b_proj_hbm,
    w_gate_hbm, out_gain_hbm, out_bias_hbm, w_out_hbm,
    out_ref,
    pair, mask, norm_gain, norm_bias, w_a_gate, w_a_proj, w_b_gate, w_b_proj, w_gate, out_gain, out_bias, w_out,
    normed, gate, x_send, x_recv, x_rows, z_send, z_recv, turned, left, right_all, product, back_z_send, back_z_recv,
    back_rows, back_x_send, back_x_recv,
    in_sem, x_ss, x_rs, z_ss, z_rs, y_ss, y_rs, back_z_ss, back_z_rs, back_x_ss, back_x_rs, ring_sem,
):
    row, col = lax.axis_index("row"), lax.axis_index("col")
    y, core = row // 4, row % 2
    x = ((row // 2) % 2) * 2 + col // 16
    z = col % 16

    def device(y, x, core, z):
        return {"row": y * 4 + (x // 2) * 2 + core, "col": (x % 2) * 16 + z}

    def remote(src, dst, ss, rs, to):
        return pltpu.make_async_remote_copy(
            src_ref=src, dst_ref=dst, send_sem=ss, recv_sem=rs, device_id=to, device_id_type=MESH
        )

    slot = core * 4 + x
    other_core = device(y, x, 1 - core, z)
    z_peers = [device(y, x, core, (z + d) % NZ) for d in FAR_FIRST]
    x_peers = [device(y, (x + dx) % NX, (core + dc) % 2, z) for dx, dc in X_AND_CORE]
    y_peers = [device((y + d) % NY, x, core, z) for d in ALONG_Y]
    barrier = pltpu.get_barrier_semaphore()
    peers = [device(y, x, core, (z + d) % NZ) for d in NEAR] + x_peers + y_peers
    for peer in peers:
        pl.semaphore_signal(barrier, inc=1, device_id=peer, device_id_type=MESH)

    loads = [
        pltpu.make_async_copy(src, dst, in_sem.at[n])
        for n, (src, dst) in enumerate(
            (
                (pair_hbm, pair), (norm_gain_hbm, norm_gain), (norm_bias_hbm, norm_bias), (w_b_gate_hbm, w_b_gate),
                (w_b_proj_hbm, w_b_proj), (mask_hbm, mask), (w_a_gate_hbm, w_a_gate), (w_a_proj_hbm, w_a_proj),
                (w_gate_hbm, w_gate), (out_gain_hbm, out_gain), (out_bias_hbm, out_bias), (w_out_hbm, w_out),
            )
        )
    ]
    for load in loads:
        load.start()
    for load in loads[:6]:
        load.wait()

    values = pair[...].astype(F32).reshape(512, 128)
    centred = values - jnp.mean(values, axis=1, keepdims=True)
    variance = jnp.mean(centred * centred, axis=1, keepdims=True)
    normed[...] = (centred * lax.rsqrt(variance + 1e-05) * norm_gain[...] + norm_bias[...]).astype(BF16)

    at_col = lax.broadcasted_iota(jnp.int32, (16, 512), 1) % 16 == lax.broadcasted_iota(jnp.int32, (16, 512), 0)
    at_row = lax.broadcasted_iota(jnp.int32, (32, 512), 1) // 16 == lax.broadcasted_iota(jnp.int32, (32, 512), 0)
    spread = lax.dot_general(
        mask[...].astype(F32).astype(BF16), at_col.astype(F32).astype(BF16), TN, preferred_element_type=F32
    )
    mask_row = jnp.sum(jnp.where(at_row, spread, 0.0), axis=0, keepdims=True)

    def project(weight):
        turned_weight = weight[...].astype(F32).T.astype(BF16)
        return lax.dot_general(turned_weight, normed[...], NT, preferred_element_type=F32)

    def edges_of(side, w_gate, w_proj):
        edges = mask_row * jax.nn.sigmoid(project(w_gate)) * project(w_proj)
        x_send[side] = edges.reshape(8, 16, 512).astype(BF16)

    def slot_at(dx, dc):
        return ((core + dc) % 2) * 4 + (x + dx + NX) % NX

    def start_along_x(side):
        copies = [
            remote(x_send.at[side, slot_at(dx, dc)], x_recv.at[side, slot], x_ss.at[side, n], x_rs.at[side, n], x_peers[n])
            for n, (dx, dc) in enumerate(X_AND_CORE)
        ]
        for copy in copies:
            copy.start()
        x_recv[side, slot] = x_send[side, slot]
        return copies

    def start_along_z(side):
        for n, (dx, dc) in enumerate(X_AND_CORE):
            arrived = x_recv.at[side, slot_at(-dx, dc)]
            remote(x_send.at[side, 0], arrived, x_ss.at[side, n], x_rs.at[side, n], x_peers[n]).wait_recv()
        for part in range(4):
            lanes = slice(part * 128, part * 128 + 128)
            x_rows[side, part] = x_recv[side, :, :, lanes].astype(F32).reshape(128, 128)
        for plane in range(NZ):
            rows = [x_rows[side, part, pl.ds(plane, 8, stride=16), :] for part in range(4)]
            z_send[side, plane] = jnp.concatenate(rows, axis=0).astype(BF16)
        copies = [
            remote(z_send.at[side, (z + d) % NZ], z_recv.at[side, d], z_ss.at[side, d], z_rs.at[side, d], z_peers[n])
            for n, d in enumerate(FAR_FIRST)
        ]
        for copy in copies:
            copy.start()
        z_recv[side, 0] = z_send[side, z]
        return copies

    def finish_along_z(side, copies):
        for copy in copies:
            copy.wait_recv()
        for half in range(2):
            blocks = swap_blocks([z_recv[side, half * 8 + a].astype(F32) for a in range(8)])
            for low in range(8):
                turned[side, half, low * 32 : low * 32 + 32, :] = blocks[low]
        result = []
        for x_low in range(2):
            halves = []
            for half in range(2):
                starts = [
                    part * 8 + of_core * 4 + x_high * 2 + x_low
                    for x_high in range(2) for of_core in range(2) for part in range(4)
                ]
                rows = [turned[side, half, pl.ds(start, 8, stride=32), :] for start in starts]
                halves.append(jnp.concatenate(rows, axis=0))
            result.append(jnp.concatenate(halves, axis=1).astype(BF16))
        return result

    edges_of(1, w_b_gate, w_b_proj)
    pl.semaphore_wait(barrier, len(peers))
    for d in (4, 12):
        pl.semaphore_signal(ring_sem, inc=1, device_id=device(y, x, core, (z + d) % NZ), device_id_type=MESH)
    right_x = start_along_x(1)
    for load in loads[6:]:
        load.wait()
    edges_of(0, w_a_gate, w_a_proj)
    left_x = start_along_x(0)
    pl.semaphore_wait(ring_sem, 2)
    right_z = start_along_z(1)
    left_z = start_along_z(0)
    gate[...] = jax.nn.sigmoid(jnp.dot(normed[...], w_gate[...], preferred_element_type=F32))

    for x_low, rows in enumerate(finish_along_z(1, right_z)):
        right_all[y, x_low] = rows
    y_copies = [
        remote(right_all.at[y], right_all.at[y], y_ss.at[d], y_rs.at[d], y_peers[n]) for n, d in enumerate(ALONG_Y)
    ]
    for copy in y_copies:
        copy.start()
    for x_low, rows in enumerate(finish_along_z(0, left_z)):
        left[x_low] = rows

    def contract(of_y):
        d = (y + NY - of_y) % NY

        @pl.when(d != 0)
        def _():
            remote(right_all.at[y], right_all.at[of_y], y_ss.at[d], y_rs.at[d], other_core).wait_recv()

        product[of_y] = lax.dot_general(left[0], right_all[of_y, 0], NT, preferred_element_type=F32) + lax.dot_general(
            left[1], right_all[of_y, 1], NT, preferred_element_type=F32
        )
        blocks = swap_blocks([product[of_y, pl.ds(low, 16, stride=8), :] for low in range(8)])
        for low in range(8):
            back_z_send[(of_y % 2) * 8 + low, of_y // 2] = blocks[low].astype(BF16)

    def back_z_copy(to_z):
        return remote(
            back_z_send.at[to_z], back_z_recv.at[z], back_z_ss.at[to_z], back_z_rs.at[z], device(y, x, core, to_z)
        )

    for odd in range(2):
        contract((y // 2) * 2 + odd)
        contract((1 - y // 2) * 2 + odd)
        for to_z in range(odd * 8, odd * 8 + 8):

            @pl.when(z != to_z)
            def _():
                back_z_copy(to_z).start()

    back_z_recv[z] = back_z_send[z]
    for d in FAR_FIRST:
        from_z = (z + NZ - d) % NZ
        remote(
            back_z_send.at[0], back_z_recv.at[from_z], back_z_ss.at[from_z], back_z_rs.at[from_z], other_core
        ).wait_recv()

    back_rows[...] = back_z_recv[...].astype(F32).reshape(512, 128)
    for to_core in range(2):
        for to_x in range(NX):
            start = (to_x % 2) * 16 + (to_x // 2) * 8 + to_core * 4
            rows = [back_rows[pl.ds(start + part, 16, stride=32), :] for part in range(4)]
            back_x_send[to_core * 4 + to_x] = jnp.concatenate(rows, axis=0).astype(BF16)
    back_x = [
        remote(back_x_send.at[slot_at(dx, dc)], back_x_recv.at[slot], back_x_ss.at[n], back_x_rs.at[n], x_peers[n])
        for n, (dx, dc) in enumerate(X_AND_CORE)
    ]
    for copy in back_x:
        copy.start()
    back_x_recv[slot] = back_x_send[slot]
    for n, (dx, dc) in enumerate(X_AND_CORE):
        arrived = back_x_recv.at[slot_at(-dx, dc)]
        remote(back_x_send.at[0], arrived, back_x_ss.at[n], back_x_rs.at[n], x_peers[n]).wait_recv()

    gain_col = jnp.broadcast_to(out_gain[...], (8, 128)).T[:, :1]
    bias_col = jnp.broadcast_to(out_bias[...], (8, 128)).T[:, :1]
    for part in range(4):
        contracted = back_x_recv[:, part * 16 : part * 16 + 16, :].astype(F32).reshape(128, 128)
        centred = contracted - jnp.mean(contracted, axis=0, keepdims=True)
        variance = jnp.mean(centred * centred, axis=0, keepdims=True)
        normed_out = (centred * lax.rsqrt(variance + 1e-05) * gain_col + bias_col).T.astype(BF16)
        result = gate[part * 128 : part * 128 + 128, :] * jnp.dot(normed_out, w_out[...], preferred_element_type=F32)
        out_ref[part * 8 : part * 8 + 8] = result.astype(BF16).reshape(8, 16, 128)

    for copy in right_x + left_x + right_z + left_z + y_copies + back_x:
        copy.wait_send()
    for d in FAR_FIRST:
        back_z_copy((z + d) % NZ).wait_send()


def per_device(
    pair, pair_mask, norm_gain, norm_bias, w_a_gate, w_a_proj, w_b_gate, w_b_proj, w_gate, out_gain, out_bias, w_out
):
    args = (
        pair, pair_mask.T, norm_gain.reshape(1, 128), norm_bias.reshape(1, 128), w_a_gate, w_a_proj, w_b_gate, w_b_proj,
        w_gate, out_gain.reshape(1, 128), out_bias.reshape(1, 128), w_out,
    )
    dma = pltpu.SemaphoreType.DMA
    return pl.pallas_call(
        kernel,
        out_shape=pltpu.VMEM(pair.shape, BF16),
        in_specs=[pl.BlockSpec(memory_space=pl.ANY)] * len(args),
        out_specs=pl.BlockSpec(memory_space=pltpu.VMEM),
        scratch_shapes=[pltpu.VMEM(a.shape, a.dtype) for a in args]
        + [
            pltpu.VMEM((512, 128), BF16),
            pltpu.VMEM((512, 128), F32),
            pltpu.VMEM((2, 8, 16, 512), BF16),
            pltpu.VMEM((2, 8, 16, 512), BF16),
            pltpu.VMEM((2, 4, 128, 128), F32),
            pltpu.VMEM((2, 16, 32, 128), BF16),
            pltpu.VMEM((2, 16, 32, 128), BF16),
            pltpu.VMEM((2, 2, 256, 128), F32),
            pltpu.VMEM((2, 128, 256), BF16),
            pltpu.VMEM((4, 2, 128, 256), BF16),
            pltpu.VMEM((4, 128, 128), F32),
            pltpu.VMEM((16, 2, 16, 128), BF16),
            pltpu.VMEM((16, 2, 16, 128), BF16),
            pltpu.VMEM((512, 128), F32),
            pltpu.VMEM((8, 64, 128), BF16),
            pltpu.VMEM((8, 64, 128), BF16),
            dma((12,)), dma((2, 7)), dma((2, 7)), dma((2, 16)), dma((2, 16)), dma((4,)), dma((4,)), dma((16,)), dma((16,)),
            dma((7,)), dma((7,)), pltpu.SemaphoreType.REGULAR,
        ],
        compiler_params=pltpu.CompilerParams(collective_id=0, has_side_effects=True, vmem_limit_bytes=32 << 20),
        name="triangle",
    )(*[pltpu.with_memory_space_constraint(a, pltpu.HBM) for a in args])


def solution(mesh):
    return jax.shard_map(
        per_device,
        mesh=mesh,
        in_specs=(P("row", "col", None), P("row", "col")) + (P(),) * 10,
        out_specs=P("row", "col", None),
        check_vma=False,
    )
```

time: 52.7 us -> 49.3 us (0.935)
  Pallas kernels: 51.9 us -> 48.5 us
    pallas_call x1, Pallas kernels: 51.9 us -> 48.5 us  [per_device(): pl.pallas_call(kernel, out_shape=pltpu.VMEM(pair.shape, BF16), in_specs=[...]
where the time goes in v3:
time: 49.3 us; the launch traced here: 49.2 us
  Pallas kernels  48.5 us (98%)
  local copies, waits for them, and re-layouts  0.66 us (1%)
    pallas_call x1, Pallas kernels, per_device(): pl.pallas_call(kernel, out_shape=pltpu.VMEM(pair.shape, BF16), in_specs=[...  48.5 us

profile of v3, /device:TPU:1, one launch (start us, length us, event | category | flops | bytes accessed | tf_op | source)
XLA Modules:
  0.0 49.2 jit_solution(11349789054809883278)
XLA Ops:
  0.0 48.5 %triangle.1 = bf16[32,16,128]{2,1,0:T(8,128)(2,1)S(1)} custom-call(bf16[32,16,128]{2,1,0:T(8,128)(2,1)} %pair_hbm.1, s32[16,32]{1,0:T(8,128)} %bitcast.5, f32[1,128]{1,0:T(1,128)} %bitcast.6, f32[1,128]{1,0:T(1,128)} %bitcast.7, bf16[128,128]{1,0:T(8,128)(2,1)} %w_a_gate_hbm.1, bf16[128,128]{1,0:T(8,128)(2,1)} %w_a_proj_hbm.1, ...), custom_call_target="tpu_custom_call" | custom-call | tf_op jit(solution)/shard_map/triangle/pallas_call | solution.py:252
  48.5 0.7 %copy.14 = bf16[32,16,128]{2,1,0:T(8,128)(2,1)} copy(bf16[32,16,128]{2,1,0:T(8,128)(2,1)S(1)} %triangle.1) | data formatting | bytes 262144

commit v4 on v3

--- a/solution.py
+++ b/solution.py
@@ -35,9 +35,10 @@
     w_gate_hbm, out_gain_hbm, out_bias_hbm, w_out_hbm,
     out_ref,
     pair, mask, norm_gain, norm_bias, w_a_gate, w_a_proj, w_b_gate, w_b_proj, w_gate, out_gain, out_bias, w_out,
-    normed, gate, x_send, x_recv, x_rows, z_send, z_recv, turned, left, right_all, product, back_z_send, back_z_recv,
-    back_rows, back_x_send, back_x_recv,
-    in_sem, x_ss, x_rs, z_ss, z_rs, y_ss, y_rs, back_z_ss, back_z_rs, back_x_ss, back_x_rs, ring_sem,
+    normed, gate, x_send, x_recv, left_rows, right_rows, left_send, left_recv, right_send, right_recv, left_turned,
+    right_turned, left, right_all, product, back_z_send, back_z_recv, back_rows, back_x_send, back_x_recv,
+    in_sem, x_ss, x_rs, left_ss, left_rs, right_ss, right_rs, y_ss, y_rs, back_z_ss, back_z_rs, back_x_ss, back_x_rs,
+    ring_sem, core_sem,
 ):
     row, col = lax.axis_index("row"), lax.axis_index("col")
     y, core = row // 4, row % 2
@@ -47,14 +48,19 @@
     def device(y, x, core, z):
         return {"row": y * 4 + (x // 2) * 2 + core, "col": (x % 2) * 16 + z}
 
+    def slot_of(x, core):
+        return (x // 2) * 4 + core * 2 + x % 2
+
+    def slot_at(dx, dc):
+        return slot_of((x + dx + NX) % NX, (core + dc) % 2)
+
     def remote(src, dst, ss, rs, to):
         return pltpu.make_async_remote_copy(
             src_ref=src, dst_ref=dst, send_sem=ss, recv_sem=rs, device_id=to, device_id_type=MESH
         )
 
-    slot = core * 4 + x
+    slot = slot_of(x, core)
     other_core = device(y, x, 1 - core, z)
-    z_peers = [device(y, x, core, (z + d) % NZ) for d in FAR_FIRST]
     x_peers = [device(y, (x + dx) % NX, (core + dc) % 2, z) for dx, dc in X_AND_CORE]
     y_peers = [device((y + d) % NY, x, core, z) for d in ALONG_Y]
     barrier = pltpu.get_barrier_semaphore()
@@ -97,110 +103,138 @@
         edges = mask_row * jax.nn.sigmoid(project(w_gate)) * project(w_proj)
         x_send[side] = edges.reshape(8, 16, 512).astype(BF16)
 
-    def slot_at(dx, dc):
-        return ((core + dc) % 2) * 4 + (x + dx + NX) % NX
-
     def start_along_x(side):
-        copies = [
-            remote(x_send.at[side, slot_at(dx, dc)], x_recv.at[side, slot], x_ss.at[side, n], x_rs.at[side, n], x_peers[n])
-            for n, (dx, dc) in enumerate(X_AND_CORE)
-        ]
-        for copy in copies:
-            copy.start()
+        for n, (dx, dc) in enumerate(X_AND_CORE):
+            remote(
+                x_send.at[side, slot_at(dx, dc)], x_recv.at[side, slot], x_ss.at[side, n], x_rs.at[side, n], x_peers[n]
+            ).start()
         x_recv[side, slot] = x_send[side, slot]
-        return copies
-
-    def start_along_z(side):
+
+    def wait_along_x(side, first_slot, slots):
         for n, (dx, dc) in enumerate(X_AND_CORE):
-            arrived = x_recv.at[side, slot_at(-dx, dc)]
-            remote(x_send.at[side, 0], arrived, x_ss.at[side, n], x_rs.at[side, n], x_peers[n]).wait_recv()
-        for part in range(4):
-            lanes = slice(part * 128, part * 128 + 128)
-            x_rows[side, part] = x_recv[side, :, :, lanes].astype(F32).reshape(128, 128)
-        for plane in range(NZ):
-            rows = [x_rows[side, part, pl.ds(plane, 8, stride=16), :] for part in range(4)]
-            z_send[side, plane] = jnp.concatenate(rows, axis=0).astype(BF16)
-        copies = [
-            remote(z_send.at[side, (z + d) % NZ], z_recv.at[side, d], z_ss.at[side, d], z_rs.at[side, d], z_peers[n])
-            for n, d in enumerate(FAR_FIRST)
-        ]
-        for copy in copies:
-            copy.start()
-        z_recv[side, 0] = z_send[side, z]
-        return copies
-
-    def finish_along_z(side, copies):
-        for copy in copies:
-            copy.wait_recv()
+            source = slot_at(-dx, dc)
+
+            def wait():
+                remote(
+                    x_send.at[side, 0], x_recv.at[side, source], x_ss.at[side, n], x_rs.at[side, n], other_core
+                ).wait_recv()
+
+            if slots == 8:
+                wait()
+            else:
+                pl.when(source // 4 == first_slot // 4)(wait)
+
+    def start_along_z(send, recv, ss, rs):
+        for d in FAR_FIRST:
+            remote(send.at[(z + d) % NZ], recv.at[d], ss.at[d], rs.at[d], device(y, x, core, (z + d) % NZ)).start()
+        recv[0] = send[z]
+
+    def finish_along_z(send, recv, ss, rs, turned, slots):
+        for d in FAR_FIRST:
+            remote(send.at[0], recv.at[d], ss.at[d], rs.at[d], other_core).wait_recv()
+        count = 4 * slots
         for half in range(2):
-            blocks = swap_blocks([z_recv[side, half * 8 + a].astype(F32) for a in range(8)])
+            blocks = swap_blocks([recv[half * 8 + a].astype(F32) for a in range(8)])
             for low in range(8):
-                turned[side, half, low * 32 : low * 32 + 32, :] = blocks[low]
+                turned[half, low * count : low * count + count, :] = blocks[low]
         result = []
         for x_low in range(2):
             halves = []
             for half in range(2):
-                starts = [
-                    part * 8 + of_core * 4 + x_high * 2 + x_low
-                    for x_high in range(2) for of_core in range(2) for part in range(4)
-                ]
-                rows = [turned[side, half, pl.ds(start, 8, stride=32), :] for start in starts]
+                starts = [part * slots + s for s in range(x_low, slots, 2) for part in range(4)]
+                rows = [turned[half, pl.ds(start, 8, stride=count), :] for start in starts]
                 halves.append(jnp.concatenate(rows, axis=0))
             result.append(jnp.concatenate(halves, axis=1).astype(BF16))
         return result
+
+    def by_plane(side, first_slot, slots, rows, send):
+        wait_along_x(side, first_slot, slots)
+        for part in range(4):
+            lanes = slice(part * 128, part * 128 + 128)
+            block = x_recv[side, first_slot : first_slot + slots, :, lanes].astype(F32).reshape(slots * 16, 128)
+            rows[part * slots * 16 : (part + 1) * slots * 16, :] = block
+        for plane in range(NZ):
+            send[plane] = rows[pl.ds(plane, 4 * slots, stride=16), :].astype(BF16)
+
+    left_z = (left_send, left_recv, left_ss, left_rs)
+    right_z = [(right_send.at[h], right_recv.at[h], right_ss.at[h], right_rs.at[h]) for h in range(2)]
+
+    def send_left():
+        by_plane(0, 0, 8, left_rows, left_send)
+        start_along_z(*left_z)
+
+    def send_right(h):
+        by_plane(1, h * 4, 4, right_rows.at[h], right_send.at[h])
+        start_along_z(*right_z[h])
 
     edges_of(1, w_b_gate, w_b_proj)
     pl.semaphore_wait(barrier, len(peers))
     for d in (4, 12):
         pl.semaphore_signal(ring_sem, inc=1, device_id=device(y, x, core, (z + d) % NZ), device_id_type=MESH)
-    right_x = start_along_x(1)
+    start_along_x(1)
     for load in loads[6:]:
         load.wait()
     edges_of(0, w_a_gate, w_a_proj)
-    left_x = start_along_x(0)
+    start_along_x(0)
     pl.semaphore_wait(ring_sem, 2)
-    right_z = start_along_z(1)
-    left_z = start_along_z(0)
+
+    def after_both_cores(send, recv, ss, rs):
+        d = FAR_FIRST[-1]
+        remote(send.at[0], recv.at[d], ss.at[d], rs.at[d], other_core).wait_send()
+        pl.semaphore_signal(core_sem, inc=1, device_id=other_core, device_id_type=MESH)
+        pl.semaphore_wait(core_sem, 1)
+
+    send_right(0)
+    send_right(1)
+    after_both_cores(*right_z[1])
+    send_left()
     gate[...] = jax.nn.sigmoid(jnp.dot(normed[...], w_gate[...], preferred_element_type=F32))
 
-    for x_low, rows in enumerate(finish_along_z(1, right_z)):
-        right_all[y, x_low] = rows
-    y_copies = [
-        remote(right_all.at[y], right_all.at[y], y_ss.at[d], y_rs.at[d], y_peers[n]) for n, d in enumerate(ALONG_Y)
-    ]
-    for copy in y_copies:
-        copy.start()
-    for x_low, rows in enumerate(finish_along_z(0, left_z)):
-        left[x_low] = rows
-
-    def contract(of_y):
-        d = (y + NY - of_y) % NY
-
-        @pl.when(d != 0)
-        def _():
-            remote(right_all.at[y], right_all.at[of_y], y_ss.at[d], y_rs.at[d], other_core).wait_recv()
-
-        product[of_y] = lax.dot_general(left[0], right_all[of_y, 0], NT, preferred_element_type=F32) + lax.dot_general(
-            left[1], right_all[of_y, 1], NT, preferred_element_type=F32
-        )
-        blocks = swap_blocks([product[of_y, pl.ds(low, 16, stride=8), :] for low in range(8)])
-        for low in range(8):
-            back_z_send[(of_y % 2) * 8 + low, of_y // 2] = blocks[low].astype(BF16)
+    def right_of(of_y, h):
+        return right_all.at[of_y % 2, h, :, pl.ds(pl.multiple_of((of_y // 2) * 64, 64), 64), :]
+
+    def y_copy(h, d, of_y):
+        return remote(right_of(y, h), right_of(of_y, h), y_ss.at[h, d], y_rs.at[h, d], device((y + d) % NY, x, core, z))
+
+    def send_along_y(h):
+        for x_low, rows in enumerate(finish_along_z(*right_z[h], right_turned.at[h], 4)):
+            right_all[y % 2, h, x_low, pl.ds(pl.multiple_of((y // 2) * 64, 64), 64), :] = rows
+        for d in ALONG_Y:
+            y_copy(h, d, y).start()
 
     def back_z_copy(to_z):
         return remote(
             back_z_send.at[to_z], back_z_recv.at[z], back_z_ss.at[to_z], back_z_rs.at[z], device(y, x, core, to_z)
         )
 
-    for odd in range(2):
-        contract((y // 2) * 2 + odd)
-        contract((1 - y // 2) * 2 + odd)
-        for to_z in range(odd * 8, odd * 8 + 8):
+    def contract(odd, h):
+        for of_y in (odd, odd + 2):
+            d = (y + NY - of_y) % NY
+
+            @pl.when(d != 0)
+            def _():
+                y_copy(h, d, of_y).wait_recv()
+
+        product[odd * 2 + h] = lax.dot_general(
+            left[0], right_all[odd, h, 0], NT, preferred_element_type=F32
+        ) + lax.dot_general(left[1], right_all[odd, h, 1], NT, preferred_element_type=F32)
+        blocks = swap_blocks([product[odd * 2 + h, pl.ds(low, 16, stride=8), :] for low in range(8)])
+        for low in range(8):
+            back_z_send[odd * 8 + h * 4 + low % 4, low // 4] = blocks[low].astype(BF16)
+        for to_z in range(odd * 8 + h * 4, odd * 8 + h * 4 + 4):
 
             @pl.when(z != to_z)
             def _():
                 back_z_copy(to_z).start()
 
+    send_along_y(0)
+    send_along_y(1)
+    for x_low, rows in enumerate(finish_along_z(*left_z, left_turned, 8)):
+        left[x_low] = rows
+    contract(0, 0)
+    contract(0, 1)
+    contract(1, 0)
+    contract(1, 1)
     back_z_recv[z] = back_z_send[z]
     for d in FAR_FIRST:
         from_z = (z + NZ - d) % NZ
@@ -213,7 +247,7 @@
         for to_x in range(NX):
             start = (to_x % 2) * 16 + (to_x // 2) * 8 + to_core * 4
             rows = [back_rows[pl.ds(start + part, 16, stride=32), :] for part in range(4)]
-            back_x_send[to_core * 4 + to_x] = jnp.concatenate(rows, axis=0).astype(BF16)
+            back_x_send[slot_of(to_x, to_core)] = jnp.concatenate(rows, axis=0).astype(BF16)
     back_x = [
         remote(back_x_send.at[slot_at(dx, dc)], back_x_recv.at[slot], back_x_ss.at[n], back_x_rs.at[n], x_peers[n])
         for n, (dx, dc) in enumerate(X_AND_CORE)
@@ -235,8 +269,23 @@
         result = gate[part * 128 : part * 128 + 128, :] * jnp.dot(normed_out, w_out[...], preferred_element_type=F32)
         out_ref[part * 8 : part * 8 + 8] = result.astype(BF16).reshape(8, 16, 128)
 
-    for copy in right_x + left_x + right_z + left_z + y_copies + back_x:
+    for copy in back_x:
         copy.wait_send()
+    for side in range(2):
+        for n in range(len(X_AND_CORE)):
+            remote(
+                x_send.at[side, 0], x_recv.at[side, 0], x_ss.at[side, n], x_rs.at[side, n], other_core
+            ).wait_send()
+    def wait_sent(send, recv, ss, rs, distances):
+        for d in distances:
+            remote(send.at[0], recv.at[d], ss.at[d], rs.at[d], other_core).wait_send()
+
+    wait_sent(*left_z, FAR_FIRST)
+    wait_sent(*right_z[0], FAR_FIRST)
+    wait_sent(*right_z[1], FAR_FIRST[:-1])
+    for h in range(2):
+        for d in ALONG_Y:
+            y_copy(h, d, y).wait_send()
     for d in FAR_FIRST:
         back_z_copy((z + d) % NZ).wait_send()
 
@@ -260,20 +309,24 @@
             pltpu.VMEM((512, 128), F32),
             pltpu.VMEM((2, 8, 16, 512), BF16),
             pltpu.VMEM((2, 8, 16, 512), BF16),
-            pltpu.VMEM((2, 4, 128, 128), F32),
-            pltpu.VMEM((2, 16, 32, 128), BF16),
-            pltpu.VMEM((2, 16, 32, 128), BF16),
-            pltpu.VMEM((2, 2, 256, 128), F32),
+            pltpu.VMEM((512, 128), F32),
+            pltpu.VMEM((2, 256, 128), F32),
+            pltpu.VMEM((16, 32, 128), BF16),
+            pltpu.VMEM((16, 32, 128), BF16),
+            pltpu.VMEM((2, 16, 16, 128), BF16),
+            pltpu.VMEM((2, 16, 16, 128), BF16),
+            pltpu.VMEM((2, 256, 128), F32),
+            pltpu.VMEM((2, 2, 128, 128), F32),
             pltpu.VMEM((2, 128, 256), BF16),
-            pltpu.VMEM((4, 2, 128, 256), BF16),
+            pltpu.VMEM((2, 2, 2, 128, 256), BF16),
             pltpu.VMEM((4, 128, 128), F32),
             pltpu.VMEM((16, 2, 16, 128), BF16),
             pltpu.VMEM((16, 2, 16, 128), BF16),
             pltpu.VMEM((512, 128), F32),
             pltpu.VMEM((8, 64, 128), BF16),
             pltpu.VMEM((8, 64, 128), BF16),
-            dma((12,)), dma((2, 7)), dma((2, 7)), dma((2, 16)), dma((2, 16)), dma((4,)), dma((4,)), dma((16,)), dma((16,)),
-            dma((7,)), dma((7,)), pltpu.SemaphoreType.REGULAR,
+            dma((12,)), dma((2, 7)), dma((2, 7)), dma((16,)), dma((16,)), dma((2, 16)), dma((2, 16)), dma((2, 4)),
+            dma((2, 4)), dma((16,)), dma((16,)), dma((7,)), dma((7,)), pltpu.SemaphoreType.REGULAR, pltpu.SemaphoreType.REGULAR,
         ],
         compiler_params=pltpu.CompilerParams(collective_id=0, has_side_effects=True, vmem_limit_bytes=32 << 20),
         name="triangle",

time: 49.3 us -> 46.9 us (0.951)
  Pallas kernels: 48.5 us -> 46.1 us
    pallas_call x1, Pallas kernels: 48.5 us -> 46.1 us  [per_device(): pl.pallas_call(kernel, out_shape=pltpu.VMEM(pair.shape, BF16), in_specs=[...]
where the time goes in v4:
time: 46.9 us; the launch traced here: 46.7 us
  Pallas kernels  46.1 us (98%)
  local copies, waits for them, and re-layouts  0.66 us (1%)
    pallas_call x1, Pallas kernels, per_device(): pl.pallas_call(kernel, out_shape=pltpu.VMEM(pair.shape, BF16), in_specs=[...  46.1 us

profile of v4, /device:TPU:1, one launch (start us, length us, event | category | flops | bytes accessed | tf_op | source)
XLA Modules:
  0.0 46.7 jit_solution(12732949122844149915)
XLA Ops:
  0.0 46.1 %triangle.1 = bf16[32,16,128]{2,1,0:T(8,128)(2,1)S(1)} custom-call(bf16[32,16,128]{2,1,0:T(8,128)(2,1)} %pair_hbm.1, s32[16,32]{1,0:T(8,128)} %bitcast.5, f32[1,128]{1,0:T(1,128)} %bitcast.6, f32[1,128]{1,0:T(1,128)} %bitcast.7, bf16[128,128]{1,0:T(8,128)(2,1)} %w_a_gate_hbm.1, bf16[128,128]{1,0:T(8,128)(2,1)} %w_a_proj_hbm.1, ...), custom_call_target="tpu_custom_call" | custom-call | tf_op jit(solution)/shard_map/triangle/pallas_call | solution.py:301
  46.1 0.7 %copy.14 = bf16[32,16,128]{2,1,0:T(8,128)(2,1)} copy(bf16[32,16,128]{2,1,0:T(8,128)(2,1)S(1)} %triangle.1) | data formatting | bytes 262144

commit v5 on v4

--- a/solution.py
+++ b/solution.py
@@ -10,6 +10,7 @@
 NZ, NX, NY = 16, 4, 4
 FAR_FIRST = (8, 7, 9, 6, 10, 5, 11, 4, 12, 3, 13, 2, 14, 1, 15)
 NEAR = (4, 12, 3, 13, 2, 14, 1, 15)
+STEP = 14
 ALONG_Y = (2, 1, 3)
 X_AND_CORE = tuple((dx, dc) for dx in (2, 1, 3, 0) for dc in (1, 0) if dx or dc)
 NT = (((1,), (1,)), ((), ()))
@@ -38,7 +39,7 @@
     normed, gate, x_send, x_recv, left_rows, right_rows, left_send, left_recv, right_send, right_recv, left_turned,
     right_turned, left, right_all, product, back_z_send, back_z_recv, back_rows, back_x_send, back_x_recv,
     in_sem, x_ss, x_rs, left_ss, left_rs, right_ss, right_rs, y_ss, y_rs, back_z_ss, back_z_rs, back_x_ss, back_x_rs,
-    ring_sem, core_sem,
+    ring_sem, core_sem, wave_sem,
 ):
     row, col = lax.axis_index("row"), lax.axis_index("col")
     y, core = row // 4, row % 2
@@ -178,15 +179,19 @@
     start_along_x(0)
     pl.semaphore_wait(ring_sem, 2)
 
+    def wait_sent(send, recv, ss, rs, distances):
+        for d in distances:
+            remote(send.at[0], recv.at[d], ss.at[d], rs.at[d], other_core).wait_send()
+
     def after_both_cores(send, recv, ss, rs):
-        d = FAR_FIRST[-1]
+        d = FAR_FIRST[STEP]
         remote(send.at[0], recv.at[d], ss.at[d], rs.at[d], other_core).wait_send()
         pl.semaphore_signal(core_sem, inc=1, device_id=other_core, device_id_type=MESH)
         pl.semaphore_wait(core_sem, 1)
 
     send_right(0)
     send_right(1)
-    after_both_cores(*right_z[1])
+    after_both_cores(*right_z[0])
     send_left()
     gate[...] = jax.nn.sigmoid(jnp.dot(normed[...], w_gate[...], preferred_element_type=F32))
 
@@ -207,7 +212,7 @@
             back_z_send.at[to_z], back_z_recv.at[z], back_z_ss.at[to_z], back_z_rs.at[z], device(y, x, core, to_z)
         )
 
-    def contract(odd, h):
+    def wait_along_y(odd, h):
         for of_y in (odd, odd + 2):
             d = (y + NY - of_y) % NY
 
@@ -215,6 +220,9 @@
             def _():
                 y_copy(h, d, of_y).wait_recv()
 
+    def contract(odd, h):
+        if odd or h:
+            wait_along_y(odd, h)
         product[odd * 2 + h] = lax.dot_general(
             left[0], right_all[odd, h, 0], NT, preferred_element_type=F32
         ) + lax.dot_general(left[1], right_all[odd, h, 1], NT, preferred_element_type=F32)
@@ -227,14 +235,41 @@
             def _():
                 back_z_copy(to_z).start()
 
-    send_along_y(0)
-    send_along_y(1)
+    @pl.when(y % 2 == 0)
+    def _():
+        send_along_y(0)
+        send_along_y(1)
+
+    wait_along_y(0, 0)
+
+    @pl.when(y % 2 == 1)
+    def _():
+        send_along_y(0)
+        send_along_y(1)
+
     for x_low, rows in enumerate(finish_along_z(*left_z, left_turned, 8)):
         left[x_low] = rows
     contract(0, 0)
+
+    first = jnp.where(z == 0, 1, 0)
+    back_z_copy(first).wait_send()
+    pl.semaphore_signal(wave_sem, inc=1, device_id=other_core, device_id_type=MESH)
+    pl.semaphore_wait(wave_sem, 1)
     contract(0, 1)
     contract(1, 0)
     contract(1, 1)
+    for side in range(2):
+        for n in range(len(X_AND_CORE)):
+            remote(
+                x_send.at[side, 0], x_recv.at[side, 0], x_ss.at[side, n], x_rs.at[side, n], other_core
+            ).wait_send()
+    wait_sent(*left_z, FAR_FIRST)
+    wait_sent(*right_z[1], FAR_FIRST)
+    wait_sent(*right_z[0], FAR_FIRST[:STEP] + FAR_FIRST[STEP + 1 :])
+    for h in range(2):
+        for d in ALONG_Y:
+            y_copy(h, d, y).wait_send()
+
     back_z_recv[z] = back_z_send[z]
     for d in FAR_FIRST:
         from_z = (z + NZ - d) % NZ
@@ -254,13 +289,16 @@
     ]
     for copy in back_x:
         copy.start()
+    gain_col = jnp.broadcast_to(out_gain[...], (8, 128)).T[:, :1]
+    bias_col = jnp.broadcast_to(out_bias[...], (8, 128)).T[:, :1]
     back_x_recv[slot] = back_x_send[slot]
+    for d in FAR_FIRST:
+        to_z = (z + d) % NZ
+        pl.when(to_z != first)(lambda: back_z_copy(to_z).wait_send())
     for n, (dx, dc) in enumerate(X_AND_CORE):
         arrived = back_x_recv.at[slot_at(-dx, dc)]
         remote(back_x_send.at[0], arrived, back_x_ss.at[n], back_x_rs.at[n], x_peers[n]).wait_recv()
 
-    gain_col = jnp.broadcast_to(out_gain[...], (8, 128)).T[:, :1]
-    bias_col = jnp.broadcast_to(out_bias[...], (8, 128)).T[:, :1]
     for part in range(4):
         contracted = back_x_recv[:, part * 16 : part * 16 + 16, :].astype(F32).reshape(128, 128)
         centred = contracted - jnp.mean(contracted, axis=0, keepdims=True)
@@ -271,23 +309,6 @@
 
     for copy in back_x:
         copy.wait_send()
-    for side in range(2):
-        for n in range(len(X_AND_CORE)):
-            remote(
-                x_send.at[side, 0], x_recv.at[side, 0], x_ss.at[side, n], x_rs.at[side, n], other_core
-            ).wait_send()
-    def wait_sent(send, recv, ss, rs, distances):
-        for d in distances:
-            remote(send.at[0], recv.at[d], ss.at[d], rs.at[d], other_core).wait_send()
-
-    wait_sent(*left_z, FAR_FIRST)
-    wait_sent(*right_z[0], FAR_FIRST)
-    wait_sent(*right_z[1], FAR_FIRST[:-1])
-    for h in range(2):
-        for d in ALONG_Y:
-            y_copy(h, d, y).wait_send()
-    for d in FAR_FIRST:
-        back_z_copy((z + d) % NZ).wait_send()
 
 
 def per_device(
@@ -327,6 +348,7 @@
             pltpu.VMEM((8, 64, 128), BF16),
             dma((12,)), dma((2, 7)), dma((2, 7)), dma((16,)), dma((16,)), dma((2, 16)), dma((2, 16)), dma((2, 4)),
             dma((2, 4)), dma((16,)), dma((16,)), dma((7,)), dma((7,)), pltpu.SemaphoreType.REGULAR, pltpu.SemaphoreType.REGULAR,
+            pltpu.SemaphoreType.REGULAR,
         ],
         compiler_params=pltpu.CompilerParams(collective_id=0, has_side_effects=True, vmem_limit_bytes=32 << 20),
         name="triangle",

time: 46.9 us -> 46.4 us (0.989)
  Pallas kernels: 46.1 us -> 45.6 us
where the time goes in v5:
time: 46.4 us; the launch traced here: 46.3 us
  Pallas kernels  45.6 us (98%)
  local copies, waits for them, and re-layouts  0.66 us (1%)
    pallas_call x1, Pallas kernels, per_device(): pl.pallas_call(kernel, out_shape=pltpu.VMEM(pair.shape, BF16), in_specs=[...  45.6 us

profile of v5, /device:TPU:1, one launch (start us, length us, event | category | flops | bytes accessed | tf_op | source)
XLA Modules:
  0.0 46.3 jit_solution(14037495495347856788)
XLA Ops:
  0.0 45.6 %triangle.1 = bf16[32,16,128]{2,1,0:T(8,128)(2,1)S(1)} custom-call(bf16[32,16,128]{2,1,0:T(8,128)(2,1)} %pair_hbm.1, s32[16,32]{1,0:T(8,128)} %bitcast.5, f32[1,128]{1,0:T(1,128)} %bitcast.6, f32[1,128]{1,0:T(1,128)} %bitcast.7, bf16[128,128]{1,0:T(8,128)(2,1)} %w_a_gate_hbm.1, bf16[128,128]{1,0:T(8,128)(2,1)} %w_a_proj_hbm.1, ...), custom_call_target="tpu_custom_call" | custom-call | tf_op jit(solution)/shard_map/triangle/pallas_call | solution.py:322
  45.6 0.7 %copy.14 = bf16[32,16,128]{2,1,0:T(8,128)(2,1)} copy(bf16[32,16,128]{2,1,0:T(8,128)(2,1)S(1)} %triangle.1) | data formatting | bytes 262144

commit v6 on v5

--- a/solution.py
+++ b/solution.py
@@ -81,13 +81,16 @@
     ]
     for load in loads:
         load.start()
-    for load in loads[:6]:
+    for load in loads[:3]:
         load.wait()
 
     values = pair[...].astype(F32).reshape(512, 128)
     centred = values - jnp.mean(values, axis=1, keepdims=True)
     variance = jnp.mean(centred * centred, axis=1, keepdims=True)
     normed[...] = (centred * lax.rsqrt(variance + 1e-05) * norm_gain[...] + norm_bias[...]).astype(BF16)
+
+    for load in loads[3:6]:
+        load.wait()
 
     at_col = lax.broadcasted_iota(jnp.int32, (16, 512), 1) % 16 == lax.broadcasted_iota(jnp.int32, (16, 512), 0)
     at_row = lax.broadcasted_iota(jnp.int32, (32, 512), 1) // 16 == lax.broadcasted_iota(jnp.int32, (32, 512), 0)
@@ -176,7 +179,6 @@
     for load in loads[6:]:
         load.wait()
     edges_of(0, w_a_gate, w_a_proj)
-    start_along_x(0)
     pl.semaphore_wait(ring_sem, 2)
 
     def wait_sent(send, recv, ss, rs, distances):
@@ -190,6 +192,7 @@
         pl.semaphore_wait(core_sem, 1)
 
     send_right(0)
+    start_along_x(0)
     send_right(1)
     after_both_cores(*right_z[0])
     send_left()

time: 46.4 us -> 45.8 us (0.987)
  Pallas kernels: 45.6 us -> 45 us
    pallas_call x1, Pallas kernels: 45.6 us -> 45 us  [per_device(): pl.pallas_call(kernel, out_shape=pltpu.VMEM(pair.shape, BF16), in_specs=[...]
where the time goes in v6:
time: 45.8 us; the launch traced here: 45.7 us
  Pallas kernels  45 us (98%)
  local copies, waits for them, and re-layouts  0.66 us (1%)
    pallas_call x1, Pallas kernels, per_device(): pl.pallas_call(kernel, out_shape=pltpu.VMEM(pair.shape, BF16), in_specs=[...  45 us

profile of v6, /device:TPU:1, one launch (start us, length us, event | category | flops | bytes accessed | tf_op | source)
XLA Modules:
  0.0 45.7 jit_solution(7281929279979331951)
XLA Ops:
  0.0 45.0 %triangle.1 = bf16[32,16,128]{2,1,0:T(8,128)(2,1)S(1)} custom-call(bf16[32,16,128]{2,1,0:T(8,128)(2,1)} %pair_hbm.1, s32[16,32]{1,0:T(8,128)} %bitcast.5, f32[1,128]{1,0:T(1,128)} %bitcast.6, f32[1,128]{1,0:T(1,128)} %bitcast.7, bf16[128,128]{1,0:T(8,128)(2,1)} %w_a_gate_hbm.1, bf16[128,128]{1,0:T(8,128)(2,1)} %w_a_proj_hbm.1, ...), custom_call_target="tpu_custom_call" | custom-call | tf_op jit(solution)/shard_map/triangle/pallas_call | solution.py:325
  45.0 0.7 %copy.14 = bf16[32,16,128]{2,1,0:T(8,128)(2,1)} copy(bf16[32,16,128]{2,1,0:T(8,128)(2,1)S(1)} %triangle.1) | data formatting | bytes 262144

commit v7 on v6

--- a/solution.py
+++ b/solution.py
@@ -11,6 +11,7 @@
 FAR_FIRST = (8, 7, 9, 6, 10, 5, 11, 4, 12, 3, 13, 2, 14, 1, 15)
 NEAR = (4, 12, 3, 13, 2, 14, 1, 15)
 STEP = 14
+EARLY = 1
 ALONG_Y = (2, 1, 3)
 X_AND_CORE = tuple((dx, dc) for dx in (2, 1, 3, 0) for dc in (1, 0) if dx or dc)
 NT = (((1,), (1,)), ((), ()))
@@ -259,8 +260,12 @@
     pl.semaphore_signal(wave_sem, inc=1, device_id=other_core, device_id_type=MESH)
     pl.semaphore_wait(wave_sem, 1)
     contract(0, 1)
-    contract(1, 0)
-    contract(1, 1)
+
+    def contract_high():
+        contract(1, 0)
+        contract(1, 1)
+
+    pl.when(z >= EARLY)(contract_high)
     for side in range(2):
         for n in range(len(X_AND_CORE)):
             remote(
@@ -295,6 +300,7 @@
     gain_col = jnp.broadcast_to(out_gain[...], (8, 128)).T[:, :1]
     bias_col = jnp.broadcast_to(out_bias[...], (8, 128)).T[:, :1]
     back_x_recv[slot] = back_x_send[slot]
+    pl.when(z < EARLY)(contract_high)
     for d in FAR_FIRST:
         to_z = (z + d) % NZ
         pl.when(to_z != first)(lambda: back_z_copy(to_z).wait_send())

time: 45.8 us -> 45.8 us (level)
  no operation moved by 1% of the time
where the time goes in v7:
time: 45.8 us; the launch traced here: 45.7 us
  Pallas kernels  45 us (98%)
  local copies, waits for them, and re-layouts  0.66 us (1%)
    pallas_call x1, Pallas kernels, per_device(): pl.pallas_call(kernel, out_shape=pltpu.VMEM(pair.shape, BF16), in_specs=[...  45 us

profile of v7, /device:TPU:1, one launch (start us, length us, event | category | flops | bytes accessed | tf_op | source)
XLA Modules:
  0.0 45.7 jit_solution(4567151227790469232)
XLA Ops:
  0.0 45.0 %triangle.1 = bf16[32,16,128]{2,1,0:T(8,128)(2,1)S(1)} custom-call(bf16[32,16,128]{2,1,0:T(8,128)(2,1)} %pair_hbm.1, s32[16,32]{1,0:T(8,128)} %bitcast.5, f32[1,128]{1,0:T(1,128)} %bitcast.6, f32[1,128]{1,0:T(1,128)} %bitcast.7, bf16[128,128]{1,0:T(8,128)(2,1)} %w_a_gate_hbm.1, bf16[128,128]{1,0:T(8,128)(2,1)} %w_a_proj_hbm.1, ...), custom_call_target="tpu_custom_call" | custom-call | tf_op jit(solution)/shard_map/triangle/pallas_call | solution.py:331
  45.0 0.7 %copy.14 = bf16[32,16,128]{2,1,0:T(8,128)(2,1)} copy(bf16[32,16,128]{2,1,0:T(8,128)(2,1)S(1)} %triangle.1) | data formatting | bytes 262144

commit v8 on v7

--- a/solution.py
+++ b/solution.py
@@ -10,7 +10,7 @@
 NZ, NX, NY = 16, 4, 4
 FAR_FIRST = (8, 7, 9, 6, 10, 5, 11, 4, 12, 3, 13, 2, 14, 1, 15)
 NEAR = (4, 12, 3, 13, 2, 14, 1, 15)
-STEP = 14
+STEP = 6
 EARLY = 1
 ALONG_Y = (2, 1, 3)
 X_AND_CORE = tuple((dx, dc) for dx in (2, 1, 3, 0) for dc in (1, 0) if dx or dc)

time: 45.8 us -> 45.9 us (level)
  no operation moved by 1% of the time
where the time goes in v8:
time: 45.9 us; the launch traced here: 45.8 us
  Pallas kernels  45.1 us (98%)
  local copies, waits for them, and re-layouts  0.66 us (1%)
    pallas_call x1, Pallas kernels, per_device(): pl.pallas_call(kernel, out_shape=pltpu.VMEM(pair.shape, BF16), in_specs=[...  45.1 us

profile of v8, /device:TPU:1, one launch (start us, length us, event | category | flops | bytes accessed | tf_op | source)
XLA Modules:
  0.0 45.8 jit_solution(14109653537162580731)
XLA Ops:
  0.0 45.1 %triangle.1 = bf16[32,16,128]{2,1,0:T(8,128)(2,1)S(1)} custom-call(bf16[32,16,128]{2,1,0:T(8,128)(2,1)} %pair_hbm.1, s32[16,32]{1,0:T(8,128)} %bitcast.5, f32[1,128]{1,0:T(1,128)} %bitcast.6, f32[1,128]{1,0:T(1,128)} %bitcast.7, bf16[128,128]{1,0:T(8,128)(2,1)} %w_a_gate_hbm.1, bf16[128,128]{1,0:T(8,128)(2,1)} %w_a_proj_hbm.1, ...), custom_call_target="tpu_custom_call" | custom-call | tf_op jit(solution)/shard_map/triangle/pallas_call | solution.py:331
  45.1 0.7 %copy.14 = bf16[32,16,128]{2,1,0:T(8,128)(2,1)} copy(bf16[32,16,128]{2,1,0:T(8,128)(2,1)S(1)} %triangle.1) | data formatting | bytes 262144
